TPU v7x, 32 devices: a whole 2x2x4 slice. The times are simulated.
32 devices in a mesh: row: 16 (over z, y, x), col: 2 (over core).
Axes of the slice: x: 2, y: 2, z: 4, core: 2. Of those that a mesh axis runs over, the one named last changes fastest.
Arguments:
- matrix: float32 [1, 2048, 8, 256], P(None, 'row', None, 'col'), may hold values from -8 to 8, as said below
Outputs:
- reduced: float32 [1, 2048, 8, 256], P(None, 'row', None, 'col')
Inputs may be any that keep to these rules, and one draw needn't show every extreme that they name: matrix holds a symmetric matrix.
All inputs are finite; a program needn't handle non-finite values.
Results may differ from a plain program's by a relative error of at most 0.0003.
Values sent between devices are 32-bit elements; how exact they have to be, the bound alone decides.
A program may use at most 64 MiB of HBM per device.

v0:
```python
import jax
import jax.numpy as jnp
from jax import lax
from jax.sharding import PartitionSpec as P


def from_root(shard, axis, root):
    mine = lax.axis_index(axis) == root
    return lax.psum(jnp.where(mine, shard, jnp.zeros_like(shard)), axis)


def product(left, right, contract):
    return lax.dot_general(
        left,
        right,
        (contract, ((), ())),
        precision=lax.Precision.HIGHEST,
        preferred_element_type=jnp.float32,
    )


def selector(tiles, width):
    identity = jnp.eye(width, dtype=jnp.float32)
    marks = (tiles == 1).astype(jnp.float32)
    return (identity[:, None, :] * marks[None, :, None]).reshape(width, tiles.shape[0] * width)


def per_device(matrix):
    row_count_tiles, width, col_count_tiles, _ = matrix.shape
    row_size = lax.axis_size("row")
    col_size = lax.axis_size("col")
    row_index = lax.axis_index("row")
    col_index = lax.axis_index("col")
    local = matrix.reshape(row_count_tiles * width, col_count_tiles * width)
    row_tiles = jnp.arange(row_count_tiles, dtype=jnp.int32) * row_size + row_index
    col_tiles = jnp.arange(col_count_tiles, dtype=jnp.int32) * col_size + col_index
    identity = jnp.eye(width, dtype=jnp.float32)
    panel = from_root(matrix[:, :, 0, :], "col", 0)
    kept = panel * (row_tiles != 0).astype(jnp.float32)[:, None, None]
    head_part = jnp.sum(panel * (row_tiles == 1).astype(jnp.float32)[:, None, None], axis=0)
    flat = kept.reshape(row_count_tiles * width, width)
    gram_part = product(flat, flat, ((0,), (0,)))
    gram, head = lax.psum((gram_part, head_part), "row")
    lower = jnp.linalg.cholesky(gram)
    basis_rows = jax.scipy.linalg.solve_triangular(lower, flat.T, lower=True)
    top_trans = jax.scipy.linalg.solve_triangular(lower, head.T, lower=True)
    shifted = identity + top_trans
    normal = product(shifted, shifted, ((0,), (0,)))
    coupling = jax.scipy.linalg.cho_solve((jnp.linalg.cholesky(normal), True), shifted.T)
    refl_rows = basis_rows + selector(row_tiles, width)
    head_tiles = from_root(matrix[0], "row", 0).reshape(width, col_count_tiles * width)
    col_mask = jnp.repeat((col_tiles != 0).astype(jnp.float32), width)
    refl_cols = jax.scipy.linalg.solve_triangular(
        lower, head_tiles * col_mask[None, :], lower=True
    ) + selector(col_tiles, width)
    image_rows = lax.psum(product(refl_cols, local, ((1,), (1,))), "col")
    image_cols = lax.psum(product(refl_rows, local, ((1,), (0,))), "row")
    middle = lax.psum(product(refl_cols, image_cols, ((1,), (1,))), "col")
    sandwich = product(coupling, product(middle, coupling, ((1,), (0,))), ((0,), (0,)))
    upd_rows = product(coupling, image_rows, ((0,), (0,))) - 0.5 * product(
        sandwich, refl_rows, ((0,), (0,))
    )
    upd_cols = product(coupling, image_cols, ((0,), (0,))) - 0.5 * product(
        sandwich, refl_cols, ((0,), (0,))
    )
    result = (
        local
        - product(upd_rows, refl_cols, ((0,), (0,)))
        - product(refl_rows, upd_cols, ((0,), (0,)))
    )
    return result.reshape(matrix.shape)


def solution(mesh):
    in_specs = (P(None, "row", None, "col"),)
    out_specs = P(None, "row", None, "col")
    return jax.shard_map(
        per_device, mesh=mesh, in_specs=in_specs, out_specs=out_specs, check_vma=False
    )
```

profile of v0, /device:TPU:0, one launch (start us, length us, event | category | flops | bytes accessed | tf_op | source)
XLA Modules:
  0.0 335.2 jit_solution(7504236610236108512)
XLA Ops:
  6.5 1.7 broadcast_select_fusion
  8.3 1.9 select_bitcast_fusion
  10.2 19.9 %all-reduce.7.cloned.1.call-done = f32[1,128,128]{2,1,0:T(8,128)} async-done(((f32[1,128,128]{2,1,0:T(8,128)}), f32[1,128,128]{2,1,0:T(8,128)}) %all-reduce.7.cloned.1.call-update) | async-done | bytes 65552 | tf_op jit(solution)/shard_map/psum | solution.py:9
  30.1 1.8 fusion.24
  32.0 1.5 multiply_bitcast_fusion
  33.4 105.3 %all-reduce.9.cloned.1.call-done = f32[128,128]{0,1:T(8,128)} async-done(((f32[128,128]{0,1:T(8,128)}), f32[128,128]{0,1:T(8,128)}) %all-reduce.9.cloned.1.call-update) | async-done | bytes 65552 | tf_op jit(solution)/shard_map/psum | solution.py:43
  138.7 0.9 copy.3
  139.6 0.9 fusion.23
  140.5 11.7 %cholesky.44 = f32[128,128]{1,0:T(8,128)S(1)} custom-call(f32[128,128]{1,0:T(8,128)S(1)} %fusion.23), custom_call_target="Cholesky" | custom-call | tf_op jit(solution)/shard_map/jit(cholesky)/cholesky | solution.py:44
  152.3 0.7 compare_reduce_fusion.1
  153.6 9.8 %custom-call.17 = f32[1,128,128]{1,2,0:T(8,128)S(1)} custom-call(f32[1,128,128]{2,1,0:T(8,128)S(1)} %fusion.11), custom_call_target="InvertDiagBlocksLowerTriangular" | custom-call | tf_op jit(solution)/shard_map/jit(_solve_triangular)/triangular_solve/custom-call.0 | solution.py:46
  163.7 1.5 fusion.5
  165.5 112.9 %all-reduce.11.cloned.1.call-done = (f32[128,128]{0,1:T(8,128)}, f32[128,8,128]{2,1,0:T(8,128)}, f32[128,1024]{1,0:T(8,128)}) async-done(((f32[128,128]{0,1:T(8,128)}, f32[128,8,128]{2,1,0:T(8,128)}, f32[128,1024]{1,0:T(8,128)}), (f32[128,128]{0,1:T(8,128)}, f32[128,8,128]{2,1,0:T(8,128)}, f32[128,1024]{1,0:T(8,128)})) %all-reduce.11.cloned.1.call-update) | async-done | bytes 1114128 | tf_op jit(solution)/shard_map/psum | solution.py:43
  278.4 1.1 convolution_add_fusion.2
  280.0 11.7 %cholesky.55 = f32[128,128]{1,0:T(8,128)S(1)} custom-call(f32[128,128]{1,0:T(8,128)S(1)} %fusion.19), custom_call_target="Cholesky" | custom-call | tf_op jit(solution)/shard_map/jit(cholesky)/cholesky | solution.py:49
  292.4 0.7 fusion.12
  293.0 9.8 %custom-call.13 = f32[1,128,128]{1,2,0:T(8,128)S(1)} custom-call(f32[1,128,128]{2,1,0:T(8,128)S(1)} %fusion.12), custom_call_target="InvertDiagBlocksLowerTriangular" | custom-call | tf_op jit(solution)/shard_map/jit(_cho_solve)/triangular_solve | solution.py:49
  303.5 0.7 convolution_add_fusion
  304.2 1.2 fusion.7
  305.4 1.2 fusion.36
  307.3 16.6 %all-reduce.13.cloned.1.call-done = (f32[128,128]{1,0:T(8,128)}, f32[128,128]{1,0:T(8,128)}) async-done(((f32[128,128]{1,0:T(8,128)}, f32[128,128]{1,0:T(8,128)}), (f32[128,128]{1,0:T(8,128)}, f32[128,128]{1,0:T(8,128)})) %all-reduce.13.cloned.1.call-update) | async-done | bytes 131088 | tf_op jit(solution)/shard_map/psum | solution.py:56
  323.8 1.2 fusion.35
  325.8 0.7 convolution_subtract_fusion.1
  327.8 0.9 copy.9
  (39 shorter events, 5.8 us)
Async XLA Ops:
  6.5 23.5 %all-reduce.7.cloned.1.call-start = ((), (), s32[]{:S(2)}) async-start(), calls=%async_computation | async-start | bytes 131072 | tf_op jit(solution)/shard_map/psum | solution.py:9
  8.3 130.4 %all-reduce.9.cloned.1.call-start = ((), (), s32[]{:S(2)}) async-start(), calls=%async_computation.1 | async-start | bytes 131072 | tf_op jit(solution)/shard_map/psum | solution.py:43
  10.2 153.5 %copy-start = (f32[1,128,8,128]{3,2,1,0:T(8,128)S(1)}, f32[1,128,8,128]{3,2,1,0:T(8,128)}, u32[]{:S(2)}) copy-start(f32[1,128,8,128]{3,2,1,0:T(8,128)} %param.4) | copy-start | bytes 1572868
  31.9 246.5 %all-reduce.11.cloned.1.call-start = ((), (), s32[]{:S(2)}) async-start(), calls=%async_computation.2 | async-start | bytes 2228224 | tf_op jit(solution)/shard_map/psum | solution.py:43
  152.9 10.5 %copy-start.2 = (f32[1,128,128]{2,1,0:T(8,128)S(1)}, f32[1,128,128]{2,1,0:T(8,128)}, u32[]{:S(2)}) copy-start(f32[1,128,128]{2,1,0:T(8,128)} %all-reduce.7.cloned.1.call-done) | copy-start | bytes 196612
  165.2 158.6 %all-reduce.13.cloned.1.call-start = ((), (), s32[]{:S(2)}) async-start(), calls=%async_computation.3 | async-start | bytes 262144 | tf_op jit(solution)/shard_map/psum | solution.py:56
  279.5 23.8 %copy-start.3 = (f32[128,8,128]{2,1,0:T(8,128)S(1)}, f32[128,8,128]{2,1,0:T(8,128)}, u32[]{:S(2)}) copy-start(f32[128,8,128]{2,1,0:T(8,128)} %get-tuple-element.8) | copy-start | bytes 1572868
  304.2 1.2 copy-start.1
  323.8 1.2 copy-start.4
Sparse Core Ops, SparseCore 0:
  9.6 20.3 all-reduce.6
  35.6 103.1 all-reduce.8
  165.3 113.0 all-reduce.10
  306.8 17.0 all-reduce.12
where the time goes:
time: 336 us; the launch traced here: 335 us
  waiting for transfers between devices  255 us (76%)
  other arithmetic  51.8 us (15%)
  between operations  13.4 us (4%)
  matrix products  13.1 us (4%)
    psum x2, waiting for transfers between devices, per_device(): gram, head = lax.psum((gram_part, head_part), 'row')  218 us
    psum x1, waiting for transfers between devices, from_root(): return lax.psum(jnp.where(mine, shard, jnp.zeros_like(shard)), axis)  19.9 us
    psum x1, waiting for transfers between devices, per_device(): image_rows = lax.psum(product(refl_cols, local, ((1,), (1,))), 'col')  16.6 us
    another operation x3, other arithmetic, per_device(): lower = jnp.linalg.cholesky(gram)  12.4 us
    another operation x3, other arithmetic, per_device(): jnp.linalg.cholesky(normal)  12.4 us
    dot_general x13, matrix products, product(): lax.dot_general(left, right, (contract, ((), ())), precision=lax.Precisio...  10.5 us
    another operation x2, other arithmetic, per_device(): top_trans = jax.scipy.linalg.solve_triangular(lower, head.T, lower=True)  10.5 us
    another operation x2, other arithmetic, per_device(): jax.scipy.linalg.cho_solve((jnp.linalg.cholesky(normal), True), shifted.T)  10.5 us
  transfers between devices with their start and end apart: 4, of which 4 were waited for; matrix products, arithmetic and copies ran while one was open for 1% of the time, Pallas kernels for 0%

commit v1 on v0

v1 whole, which is shorter than its diff:
```python
import functools

import jax
import jax.numpy as jnp
from jax import lax
from jax.experimental import pallas as pl
from jax.experimental.pallas import tpu as pltpu
from jax.sharding import PartitionSpec as P

MESH = pl.DeviceIdType.MESH
VMEM_LIMIT = 48 * 1024 * 1024


def product(left, right, contract):
    return lax.dot_general(
        left,
        right,
        (contract, ((), ())),
        precision=lax.Precision.HIGHEST,
        preferred_element_type=jnp.float32,
    )


TN = ((0,), (0,))
NN = ((1,), (0,))
NT = ((1,), (1,))


def exchange_start(source, slots, send_sem, recv_sem, cols):
    c = lax.axis_index("col")
    r = lax.axis_index("row")
    copies = []
    for step in range(1, cols):
        copy = pltpu.make_async_remote_copy(
            src_ref=source,
            dst_ref=slots.at[step - 1],
            send_sem=send_sem.at[step - 1],
            recv_sem=recv_sem.at[step - 1],
            device_id=(r, lax.rem(c + step, cols)),
            device_id_type=MESH,
        )
        copy.start()
        copies.append(copy)
    return copies


def spread(source, dest, slot, rows, target_col, send_sem, recv_sem, wait):
    r = lax.axis_index("row")

    def body(step, carry):
        copy = pltpu.make_async_remote_copy(
            src_ref=source,
            dst_ref=dest.at[slot],
            send_sem=send_sem.at[step],
            recv_sem=recv_sem.at[slot],
            device_id=(lax.rem(r + step, rows), target_col),
            device_id_type=MESH,
        )
        if wait:
            copy.wait_send()
        else:
            copy.start()
        return carry

    lax.fori_loop(1, rows, body, 0)


def arrive(source, dest, slot, recv_sem):
    pltpu.make_async_remote_copy(
        src_ref=source,
        dst_ref=dest.at[slot],
        send_sem=recv_sem.at[slot],
        recv_sem=recv_sem.at[slot],
        device_id=(lax.axis_index("row"), lax.axis_index("col")),
        device_id_type=MESH,
    ).wait_recv()


def greet(rows, cols, root_col, sends):
    r = lax.axis_index("row")
    c = lax.axis_index("col")
    barrier = pltpu.get_barrier_semaphore()

    def body(slot, carry):
        root = slot * cols + c

        @pl.when(root != r)
        def _():
            pl.semaphore_signal(barrier, inc=1, device_id=(root, root_col), device_id_type=MESH)

        return carry

    lax.fori_loop(0, rows // cols, body, 0)
    for step in range(1, cols):
        pl.semaphore_signal(
            barrier, inc=1, device_id=(r, lax.rem(c + step, cols)), device_id_type=MESH
        )

    @pl.when(sends)
    def _():
        pl.semaphore_wait(barrier, rows - 1 + cols - 1)

    @pl.when(jnp.logical_not(sends))
    def _():
        pl.semaphore_wait(barrier, cols - 1)


def gather_kernel(
    rows, cols, local_ref, tiles_ref, own_ref, sums_ref,
    parts, slots, send_sem, recv_sem, own_send, own_recv, ex_send, ex_recv,
):
    r = lax.axis_index("row")
    c = lax.axis_index("col")
    is_root = c == 0
    count = rows // cols
    slot_own = r // cols
    own_col = lax.rem(r, cols)

    @pl.when(is_root)
    def _():
        own_ref[...] = local_ref[0, :, 0, :]

    greet(rows, cols, 0, is_root)

    @pl.when(is_root)
    def _():
        for peer in range(1, cols):
            pltpu.make_async_remote_copy(
                src_ref=own_ref, dst_ref=own_ref, send_sem=own_send.at[peer - 1],
                recv_sem=own_recv, device_id=(r, peer), device_id_type=MESH,
            ).start()
        spread(own_ref, tiles_ref, slot_own, rows, own_col, send_sem, recv_sem, False)

    @pl.when(jnp.logical_not(is_root))
    def _():
        pltpu.make_async_remote_copy(
            src_ref=own_ref, dst_ref=own_ref, send_sem=own_recv,
            recv_sem=own_recv, device_id=(r, c), device_id_type=MESH,
        ).wait_recv()

    @pl.when(own_col == c)
    def _():
        tiles_ref[slot_own] = own_ref[...]

    parts[...] = jnp.zeros_like(parts)

    def gram_step(slot, carry):
        tile = slot * cols + c

        @pl.when(tile != r)
        def _():
            arrive(own_ref, tiles_ref, slot, recv_sem)

        @pl.when(tile != 0)
        def _():
            block = tiles_ref[slot]
            parts[0] += product(block, block, TN)

        @pl.when(tile == 1)
        def _():
            parts[1] = tiles_ref[slot]

        return carry

    lax.fori_loop(0, count, gram_step, 0)
    copies = exchange_start(parts, slots, ex_send, ex_recv, cols)
    for copy in copies:
        copy.wait()
    total = parts[...]
    for step in range(cols - 1):
        total = total + slots[step]
    sums_ref[...] = total

    @pl.when(is_root)
    def _():
        for peer in range(1, cols):
            pltpu.make_async_remote_copy(
                src_ref=own_ref, dst_ref=own_ref, send_sem=own_send.at[peer - 1],
                recv_sem=own_recv, device_id=(r, peer), device_id_type=MESH,
            ).wait_send()
        spread(own_ref, tiles_ref, slot_own, rows, own_col, send_sem, recv_sem, True)


def image_kernel(
    rows, cols, local_ref, vec_ref, image_ref, own_ref, middle_ref,
    part, slots, mid, mid_slots, send_sem, recv_sem, ex_send, ex_recv, mid_send, mid_recv,
):
    r = lax.axis_index("row")
    c = lax.axis_index("col")
    count = rows // cols
    slot_own = r // cols
    sends = lax.rem(r, cols) == c
    total = product(local_ref[0, :, 0, :], vec_ref[0], NN)
    for slot in range(1, count):
        total = total + product(local_ref[0, :, slot, :], vec_ref[slot], NN)
    part[...] = total
    greet(rows, cols, c, sends)
    copies = exchange_start(part, slots, ex_send, ex_recv, cols)
    for copy in copies:
        copy.wait()
    total = part[...]
    for step in range(cols - 1):
        total = total + slots[step]
    own_ref[...] = total

    @pl.when(sends)
    def _():
        spread(own_ref, image_ref, slot_own, rows, c, send_sem, recv_sem, False)
        image_ref[slot_own] = total

    mid[...] = jnp.zeros_like(mid)

    def mid_step(slot, carry):
        @pl.when(slot * cols + c != r)
        def _():
            arrive(own_ref, image_ref, slot, recv_sem)

        mid[...] += product(vec_ref[slot], image_ref[slot], TN)
        return carry

    lax.fori_loop(0, count, mid_step, 0)
    copies = exchange_start(mid, mid_slots, mid_send, mid_recv, cols)
    for copy in copies:
        copy.wait()
    total = mid[...]
    for step in range(cols - 1):
        total = total + mid_slots[step]
    middle_ref[...] = total

    @pl.when(sends)
    def _():
        spread(own_ref, image_ref, slot_own, rows, c, send_sem, recv_sem, True)


def vmem(count):
    return [pl.BlockSpec(memory_space=pltpu.VMEM)] * count


def f32(*shape):
    return jax.ShapeDtypeStruct(shape, jnp.float32)


def gather_panel(matrix, rows, cols):
    _, width, count, _ = matrix.shape
    dma = pltpu.SemaphoreType.DMA
    return pl.pallas_call(
        functools.partial(gather_kernel, rows, cols),
        out_shape=(f32(count, width, width), f32(width, width), f32(2, width, width)),
        in_specs=vmem(1),
        out_specs=tuple(vmem(3)),
        scratch_shapes=[
            pltpu.VMEM((2, width, width), jnp.float32),
            pltpu.VMEM((cols - 1, 2, width, width), jnp.float32),
            dma((rows,)), dma((count,)), dma((cols - 1,)), dma,
            dma((cols - 1,)), dma((cols - 1,)),
        ],
        compiler_params=pltpu.CompilerParams(
            collective_id=0, has_side_effects=True, vmem_limit_bytes=VMEM_LIMIT
        ),
    )(matrix)


def gather_image(matrix, vectors, rows, cols):
    _, width, count, _ = matrix.shape
    dma = pltpu.SemaphoreType.DMA
    return pl.pallas_call(
        functools.partial(image_kernel, rows, cols),
        out_shape=(f32(count, width, width), f32(width, width), f32(width, width)),
        in_specs=vmem(2),
        out_specs=tuple(vmem(3)),
        scratch_shapes=[
            pltpu.VMEM((width, width), jnp.float32),
            pltpu.VMEM((cols - 1, width, width), jnp.float32),
            pltpu.VMEM((width, width), jnp.float32),
            pltpu.VMEM((cols - 1, width, width), jnp.float32),
            dma((rows,)), dma((count,)), dma((cols - 1,)), dma((cols - 1,)),
            dma((cols - 1,)), dma((cols - 1,)),
        ],
        compiler_params=pltpu.CompilerParams(
            collective_id=1, has_side_effects=True, vmem_limit_bytes=VMEM_LIMIT
        ),
    )(matrix, vectors)


def per_device(matrix):
    _, width, count, _ = matrix.shape
    rows = lax.axis_size("row")
    cols = lax.axis_size("col")
    r = lax.axis_index("row")
    c = lax.axis_index("col")
    col_tiles = jnp.arange(count, dtype=jnp.int32) * cols + c
    identity = jnp.eye(width, dtype=jnp.float32)
    tiles, own, sums = gather_panel(matrix, rows, cols)
    gram, head = sums[0], sums[1]
    lower = jnp.linalg.cholesky(gram)
    inverse = jax.scipy.linalg.solve_triangular(lower, identity, lower=True)
    shifted = identity + product(inverse, head, NT)
    normal = product(shifted, shifted, TN)
    coupling = jax.scipy.linalg.cho_solve((jnp.linalg.cholesky(normal), True), shifted.T)
    row_vec = jnp.where(r != 0, product(own, inverse, NT), 0.0) + jnp.where(r == 1, identity, 0.0)
    col_vec = product(tiles.reshape(count * width, width), inverse, NT).reshape(tiles.shape)
    col_vec = jnp.where((col_tiles != 0)[:, None, None], col_vec, 0.0) + jnp.where(
        (col_tiles == 1)[:, None, None], identity, 0.0
    )
    image, own_image, middle = gather_image(matrix, col_vec, rows, cols)
    sandwich = product(coupling, product(middle, coupling, NN), TN)
    flat_vec = col_vec.reshape(count * width, width)
    flat_image = image.reshape(count * width, width)
    upd_rows = product(own_image, coupling, NN) - 0.5 * product(row_vec, sandwich, NN)
    upd_cols = product(flat_image, coupling, NN) - 0.5 * product(flat_vec, sandwich, NN)
    left = jnp.concatenate([upd_rows, row_vec], axis=1)
    right = jnp.concatenate([flat_vec, upd_cols], axis=1)
    change = product(left, right, NT)
    return matrix - change.reshape(matrix.shape)


def solution(mesh):
    in_specs = (P(None, "row", None, "col"),)
    out_specs = P(None, "row", None, "col")
    return jax.shard_map(
        per_device, mesh=mesh, in_specs=in_specs, out_specs=out_specs, check_vma=False
    )
```

time: 336 us -> 97.3 us (0.29)
  the two profiles are of different devices: /device:TPU:0 before, /device:TPU:31 now
where the time goes in v1:
time: 97.3 us; the launch traced here: 97.1 us
  other arithmetic  46.9 us (48%)
  Pallas kernels  43.1 us (44%)
  matrix products  5.06 us (5%)
  local copies, waits for them, and re-layouts  1.78 us (2%)
    pallas_call x1, Pallas kernels, gather_image(): pl.pallas_call(functools.partial(image_kernel, rows, cols), out_shape=(f3...  22.1 us
    pallas_call x1, Pallas kernels, gather_panel(): pl.pallas_call(functools.partial(gather_kernel, rows, cols), out_shape=(f...  21 us
    another operation x3, other arithmetic, per_device(): lower = jnp.linalg.cholesky(gram)  12.4 us
    another operation x3, other arithmetic, per_device(): jnp.linalg.cholesky(normal)  12.4 us
    another operation x2, other arithmetic, per_device(): jax.scipy.linalg.cho_solve((jnp.linalg.cholesky(normal), True), shifted.T)  10.6 us
    another operation x2, other arithmetic, per_device(): inverse = jax.scipy.linalg.solve_triangular(lower, identity, lower=True)  10.5 us
    dot_general x11, matrix products, product(): lax.dot_general(left, right, (contract, ((), ())), precision=lax.Precisio...  4.29 us

profile of v1, /device:TPU:31, one launch (start us, length us, event | category | flops | bytes accessed | tf_op | source)
XLA Modules:
  0.0 97.1 jit_solution(17318065689624873231)
XLA Ops:
  0.4 0.8 copy-done
  1.3 21.0 %shard_map.17 = (f32[8,128,128]{2,1,0:T(8,128)S(1)}, f32[128,128]{1,0:T(8,128)S(1)}, f32[2,128,128]{2,1,0:T(8,128)S(1)}) custom-call(f32[1,128,8,128]{3,2,1,0:T(8,128)S(1)} %copy-done), custom_call_target="tpu_custom_call" | custom-call | tf_op jit(solution)/shard_map/pallas_call | solution.py:246
  22.5 11.7 %cholesky.44 = f32[128,128]{1,0:T(8,128)S(1)} custom-call(f32[128,128]{1,0:T(8,128)S(1)} %fusion.15), custom_call_target="Cholesky" | custom-call | tf_op jit(solution)/shard_map/jit(cholesky)/cholesky | solution.py:295
  34.2 0.6 compare_reduce_fusion.1
  34.9 0.7 fusion.13
  35.5 9.8 %custom-call.11 = f32[1,128,128]{1,2,0:T(8,128)S(1)} custom-call(f32[1,128,128]{2,1,0:T(8,128)S(1)} %fusion.13), custom_call_target="InvertDiagBlocksLowerTriangular" | custom-call | tf_op jit(solution)/shard_map/jit(_solve_triangular)/triangular_solve/custom-call.0 | solution.py:296
  45.3 0.3 fusion.10
  45.6 0.3 fusion.21
  45.9 0.6 select_add_fusion
  46.5 0.3 fusion.3
  47.1 0.3 fusion.12
  47.5 11.7 %cholesky.55 = f32[128,128]{1,0:T(8,128)S(1)} custom-call(f32[128,128]{1,0:T(8,128)S(1)} %fusion.20), custom_call_target="Cholesky" | custom-call | tf_op jit(solution)/shard_map/jit(cholesky)/cholesky | solution.py:299
  59.3 0.6 compare_reduce_fusion
  59.9 0.7 fusion.14
  60.6 10.0 %custom-call.9 = f32[1,128,128]{1,2,0:T(8,128)S(1)} custom-call(f32[1,128,128]{2,1,0:T(8,128)S(1)} %fusion.14), custom_call_target="InvertDiagBlocksLowerTriangular" | custom-call | tf_op jit(solution)/shard_map/jit(_cho_solve)/triangular_solve | solution.py:299
  70.6 0.3 fusion.16
  70.9 0.2 fusion.18
  71.1 22.1 %shard_map.18 = (f32[8,128,128]{2,1,0:T(8,128)S(1)}, f32[128,128]{1,0:T(8,128)S(1)}, f32[128,128]{1,0:T(8,128)S(1)}) custom-call(f32[1,128,8,128]{3,2,1,0:T(8,128)S(1)} %copy-done, f32[8,128,128]{2,1,0:T(8,128)S(1)} %select_add_fusion.1.vec_ref), custom_call_target="tpu_custom_call" | custom-call | tf_op jit(solution)/shard_map/pallas_call | solution.py:266
  93.6 0.3 fusion.32
  93.9 0.6 fusion.33
  94.6 0.6 fusion
  95.2 0.2 fusion.1
  95.4 0.7 convolution_bitcast_fusion
  96.2 0.9 bitcast_subtract_fusion
  (20 shorter events, 1.6 us)
Async XLA Ops:
  0.2 1.0 %copy-start = (f32[1,128,8,128]{3,2,1,0:T(8,128)S(1)}, f32[1,128,8,128]{3,2,1,0:T(8,128)}, u32[]{:S(2)}) copy-start(f32[1,128,8,128]{3,2,1,0:T(8,128)} %local_ref.3) | copy-start | bytes 1572868

commit v2 on v1

--- a/solution.py
+++ b/solution.py
@@ -230,6 +230,102 @@
     @pl.when(sends)
     def _():
         spread(own_ref, image_ref, slot_own, rows, c, send_sem, recv_sem, True)
+
+
+BLOCK = 16
+
+
+def columns_of(block):
+    size, lanes = block.shape[0], 128
+    return [jnp.broadcast_to(block[:, j : j + 1], (size, lanes)) for j in range(size)]
+
+
+def small_cholesky_inverse(block):
+    size = block.shape[0]
+    cols = columns_of(block)
+    row = lax.broadcasted_iota(jnp.int32, (size, 128), 0)
+    lane = lax.broadcasted_iota(jnp.int32, (size, 128), 1)
+    inv = (row == lane).astype(jnp.float32)
+    for j in range(size):
+        scale = lax.rsqrt(cols[j][j : j + 1])
+        factor = cols[j] * scale
+        for k in range(j + 1, size):
+            cols[k] = cols[k] - factor * factor[k : k + 1]
+        pivot = inv[j : j + 1] * scale
+        below = jnp.where(row > j, factor, 0.0)
+        inv = jnp.where(row == j, pivot, inv - below * pivot)
+    return inv[:, :size]
+
+
+def small_inverse(block):
+    size = block.shape[0]
+    cols = columns_of(block)
+    row = lax.broadcasted_iota(jnp.int32, (size, 128), 0)
+    lane = lax.broadcasted_iota(jnp.int32, (size, 128), 1)
+    inv = (row == lane).astype(jnp.float32)
+    for j in range(size):
+        scale = 1.0 / cols[j][j : j + 1]
+        others = jnp.where(row == j, 0.0, cols[j])
+        for k in range(j + 1, size):
+            pivot = cols[k][j : j + 1] * scale
+            cols[k] = jnp.where(row == j, pivot, cols[k] - others * pivot)
+        pivot = inv[j : j + 1] * scale
+        inv = jnp.where(row == j, pivot, inv - others * pivot)
+    return inv[:, :size]
+
+
+def unit(width):
+    row = lax.broadcasted_iota(jnp.int32, (width, width), 0)
+    lane = lax.broadcasted_iota(jnp.int32, (width, width), 1)
+    return (row == lane).astype(jnp.float32)
+
+
+def cholesky_inverse(gram):
+    width = gram.shape[0]
+    step = min(BLOCK, width)
+    rest = jnp.concatenate([gram, unit(width)], axis=1)
+    done = []
+    for start in range(0, width, step):
+        small = small_cholesky_inverse(rest[:step, start : start + step])
+        lead = product(small, rest[:step], NN)
+        done.append(lead[:, width:])
+        if start + step < width:
+            rest = rest[step:] - product(lead[:, start + step : width], lead, TN)
+    return jnp.concatenate(done, axis=0)
+
+
+def full_inverse(matrix):
+    width = matrix.shape[0]
+    step = min(BLOCK, width)
+    work = jnp.concatenate([matrix, unit(width)], axis=1)
+    row = lax.broadcasted_iota(jnp.int32, (width, step), 0)
+    for start in range(0, width, step):
+        stop = start + step
+        small = small_inverse(work[start:stop, start:stop])
+        lead = product(small, work[start:stop], NN)
+        inside = jnp.logical_and(row >= start, row < stop)
+        work = work - product(jnp.where(inside, 0.0, work[:, start:stop]), lead, NN)
+        pieces = [work[:start], lead, work[stop:]]
+        work = jnp.concatenate([piece for piece in pieces if piece.shape[0]], axis=0)
+    return work[:, width:]
+
+
+def factor_kernel(rows, cols, sums_ref, own_ref, tiles_ref, row_ref, vec_ref, coupling_ref):
+    r = lax.axis_index("row")
+    c = lax.axis_index("col")
+    width = own_ref.shape[0]
+    identity = unit(width)
+    inverse = cholesky_inverse(sums_ref[0])
+
+    def vectors(tile, block):
+        keep = (tile != 0).astype(jnp.float32)
+        first = (tile == 1).astype(jnp.float32)
+        return product(block, inverse, NT) * keep + identity * first
+
+    row_ref[...] = vectors(r, own_ref[...])
+    for slot in range(rows // cols):
+        vec_ref[slot] = vectors(slot * cols + c, tiles_ref[slot])
+    coupling_ref[...] = full_inverse(identity + product(inverse, sums_ref[1], NT))
 
 
 def vmem(count):
@@ -282,26 +378,23 @@
     )(matrix, vectors)
 
 
+def factor(sums, own, tiles, rows, cols):
+    width = own.shape[0]
+    return pl.pallas_call(
+        functools.partial(factor_kernel, rows, cols),
+        out_shape=(f32(width, width), f32(*tiles.shape), f32(width, width)),
+        in_specs=vmem(3),
+        out_specs=tuple(vmem(3)),
+        compiler_params=pltpu.CompilerParams(vmem_limit_bytes=VMEM_LIMIT),
+    )(sums, own, tiles)
+
+
 def per_device(matrix):
     _, width, count, _ = matrix.shape
     rows = lax.axis_size("row")
     cols = lax.axis_size("col")
-    r = lax.axis_index("row")
-    c = lax.axis_index("col")
-    col_tiles = jnp.arange(count, dtype=jnp.int32) * cols + c
-    identity = jnp.eye(width, dtype=jnp.float32)
     tiles, own, sums = gather_panel(matrix, rows, cols)
-    gram, head = sums[0], sums[1]
-    lower = jnp.linalg.cholesky(gram)
-    inverse = jax.scipy.linalg.solve_triangular(lower, identity, lower=True)
-    shifted = identity + product(inverse, head, NT)
-    normal = product(shifted, shifted, TN)
-    coupling = jax.scipy.linalg.cho_solve((jnp.linalg.cholesky(normal), True), shifted.T)
-    row_vec = jnp.where(r != 0, product(own, inverse, NT), 0.0) + jnp.where(r == 1, identity, 0.0)
-    col_vec = product(tiles.reshape(count * width, width), inverse, NT).reshape(tiles.shape)
-    col_vec = jnp.where((col_tiles != 0)[:, None, None], col_vec, 0.0) + jnp.where(
-        (col_tiles == 1)[:, None, None], identity, 0.0
-    )
+    row_vec, col_vec, coupling = factor(sums, own, tiles, rows, cols)
     image, own_image, middle = gather_image(matrix, col_vec, rows, cols)
     sandwich = product(coupling, product(middle, coupling, NN), TN)
     flat_vec = col_vec.reshape(count * width, width)

time: 97.3 us -> 61.4 us (0.63)
  other arithmetic: 46.9 us -> 0.87 us
  Pallas kernels: 43.1 us -> 55.9 us
  matrix products: 5.06 us -> 3.23 us
    another operation x10 -> x0, other arithmetic: 45.9 us -> none  [the longest x3 12.4 us: per_device(): lower = jnp.linalg.cholesky(gram)]
    pallas_call x0 -> x1, Pallas kernels: none -> 12.8 us  [factor(): pl.pallas_call(functools.partial(factor_kernel, rows, cols), out_shape=(f...]
    dot_general x11 -> x7, matrix products: 4.29 us -> 3.23 us  [product(): lax.dot_general(left, right, (contract, ((), ())), precision=lax.Precisio...]
where the time goes in v2:
time: 61.4 us; the launch traced here: 61.2 us
  Pallas kernels  55.9 us (91%)
  matrix products  3.23 us (5%)
  local copies, waits for them, and re-layouts  1.14 us (2%)
  other arithmetic  0.87 us (1%)
    pallas_call x1, Pallas kernels, gather_image(): pl.pallas_call(functools.partial(image_kernel, rows, cols), out_shape=(f3...  22.1 us
    pallas_call x1, Pallas kernels, gather_panel(): pl.pallas_call(functools.partial(gather_kernel, rows, cols), out_shape=(f...  21 us
    pallas_call x1, Pallas kernels, factor(): pl.pallas_call(functools.partial(factor_kernel, rows, cols), out_shape=(f...  12.8 us
    dot_general x7, matrix products, product(): lax.dot_general(left, right, (contract, ((), ())), precision=lax.Precisio...  3.23 us

profile of v2, /device:TPU:31, one launch (start us, length us, event | category | flops | bytes accessed | tf_op | source)
XLA Modules:
  0.0 61.2 jit_solution(16140430864339133721)
XLA Ops:
  0.0 0.0 copy-start
  0.0 1.0 %copy-done = f32[1,128,8,128]{3,2,1,0:T(8,128)S(1)} copy-done((f32[1,128,8,128]{3,2,1,0:T(8,128)S(1)}, f32[1,128,8,128]{3,2,1,0:T(8,128)}, u32[]{:S(2)}) %copy-start) | copy-done | bytes 524312
  1.0 0.0 copy-start.1
  1.0 21.0 %shard_map.17 = (f32[8,128,128]{2,1,0:T(8,128)S(1)}, f32[128,128]{1,0:T(8,128)S(1)}, f32[2,128,128]{2,1,0:T(8,128)S(1)}) custom-call(f32[1,128,8,128]{3,2,1,0:T(8,128)S(1)} %copy-done), custom_call_target="tpu_custom_call" | custom-call | tf_op jit(solution)/shard_map/pallas_call | solution.py:342
  22.0 12.8 %shard_map.18 = (f32[128,128]{1,0:T(8,128)S(1)}, f32[8,128,128]{2,1,0:T(8,128)S(1)}, f32[128,128]{1,0:T(8,128)S(1)}) custom-call(f32[2,128,128]{2,1,0:T(8,128)S(1)} %get-tuple-element.14.sums_ref, f32[128,128]{1,0:T(8,128)S(1)} %get-tuple-element.15.own_ref, f32[8,128,128]{2,1,0:T(8,128)S(1)} %get-tuple-element.16.tiles_ref), custom_call_target="tpu_custom_call" | custom-call | tf_op jit(solution)/shard_map/pallas_call | solution.py:383
  34.8 0.0 copy-done.1
  34.8 22.1 %shard_map.19 = (f32[8,128,128]{2,1,0:T(8,128)S(1)}, f32[128,128]{1,0:T(8,128)S(1)}, f32[128,128]{1,0:T(8,128)S(1)}) custom-call(f32[1,128,8,128]{3,2,1,0:T(8,128)S(1)} %copy-done.1, f32[8,128,128]{2,1,0:T(8,128)S(1)} %get-tuple-element.17.vec_ref), custom_call_target="tpu_custom_call" | custom-call | tf_op jit(solution)/shard_map/pallas_call | solution.py:362
  57.0 0.2 fusion.9
  57.2 0.2 fusion.10
  57.4 0.3 fusion.11
  57.7 0.6 fusion.12
  58.3 0.6 fusion
  58.8 0.2 fusion.1
  59.0 1.2 %convolution_bitcast_fusion = f32[16,8,8,128]{3,1,2,0:T(8,128)S(1)} fusion(f32[1024,128]{1,0:T(8,128)S(1)} %fusion, f32[1024,128]{1,0:T(8,128)S(1)} %bitcast.21, f32[128,128]{1,0:T(8,128)S(1)} %get-tuple-element.20, f32[128,128]{1,0:T(8,128)S(1)} %fusion.1), kind=kOutput, calls=%fused_computation | convolution fusion | flops 402948096 | bytes 1703936 | tf_op jit(solution)/shard_map/dot_general | solution.py:15
  60.3 0.1 copy.2
  60.4 0.9 %bitcast_subtract_fusion = f32[1,128,8,128]{3,2,1,0:T(8,128)} fusion(f32[1,128,8,128]{3,2,1,0:T(8,128)S(1)} %copy-done.1, f32[1,128,8,128]{3,2,1,0:T(8,128)S(1)} %bitcast.23), kind=kLoop, calls=%fused_computation.8 | loop fusion | flops 131072 | bytes 1572864 | tf_op jit(solution)/shard_map/sub | solution.py:407
Async XLA Ops:
  0.0 1.0 %copy-start = (f32[1,128,8,128]{3,2,1,0:T(8,128)S(1)}, f32[1,128,8,128]{3,2,1,0:T(8,128)}, u32[]{:S(2)}) copy-start(f32[1,128,8,128]{3,2,1,0:T(8,128)} %local_ref.3) | copy-start | bytes 1572868
  1.0 33.8 %copy-start.1 = (f32[1,128,8,128]{3,2,1,0:T(8,128)S(1)}, f32[1,128,8,128]{3,2,1,0:T(8,128)}, u32[]{:S(2)}) copy-start(f32[1,128,8,128]{3,2,1,0:T(8,128)} %local_ref.3) | copy-start | bytes 1572868

commit v3 on v1

v3 whole, which is shorter than its diff:
```python
import functools

import jax
import jax.numpy as jnp
from jax import lax
from jax.experimental import pallas as pl
from jax.experimental.pallas import tpu as pltpu
from jax.sharding import PartitionSpec as P

MESH = pl.DeviceIdType.MESH
VMEM_LIMIT = 48 * 1024 * 1024


def product(left, right, contract):
    return lax.dot_general(
        left,
        right,
        (contract, ((), ())),
        precision=lax.Precision.HIGHEST,
        preferred_element_type=jnp.float32,
    )


TN = ((0,), (0,))
NN = ((1,), (0,))
NT = ((1,), (1,))


def exchange_start(source, slots, send_sem, recv_sem, cols):
    c = lax.axis_index("col")
    r = lax.axis_index("row")
    copies = []
    for step in range(1, cols):
        copy = pltpu.make_async_remote_copy(
            src_ref=source,
            dst_ref=slots.at[step - 1],
            send_sem=send_sem.at[step - 1],
            recv_sem=recv_sem.at[step - 1],
            device_id=(r, lax.rem(c + step, cols)),
            device_id_type=MESH,
        )
        copy.start()
        copies.append(copy)
    return copies


def spread(source, dest, slot, rows, target_col, send_sem, recv_sem, wait):
    r = lax.axis_index("row")

    def body(step, carry):
        copy = pltpu.make_async_remote_copy(
            src_ref=source,
            dst_ref=dest.at[slot],
            send_sem=send_sem.at[step],
            recv_sem=recv_sem.at[slot],
            device_id=(lax.rem(r + step, rows), target_col),
            device_id_type=MESH,
        )
        if wait:
            copy.wait_send()
        else:
            copy.start()
        return carry

    lax.fori_loop(1, rows, body, 0)


def arrive(source, dest, slot, recv_sem):
    pltpu.make_async_remote_copy(
        src_ref=source,
        dst_ref=dest.at[slot],
        send_sem=recv_sem.at[slot],
        recv_sem=recv_sem.at[slot],
        device_id=(lax.axis_index("row"), lax.axis_index("col")),
        device_id_type=MESH,
    ).wait_recv()


BLOCK = 16


def columns_of(block):
    size, lanes = block.shape[0], 128
    return [jnp.broadcast_to(block[:, j : j + 1], (size, lanes)) for j in range(size)]


def small_cholesky_inverse(block):
    size = block.shape[0]
    cols = columns_of(block)
    row = lax.broadcasted_iota(jnp.int32, (size, 128), 0)
    lane = lax.broadcasted_iota(jnp.int32, (size, 128), 1)
    inv = (row == lane).astype(jnp.float32)
    for j in range(size):
        scale = lax.rsqrt(cols[j][j : j + 1])
        factor = cols[j] * scale
        for k in range(j + 1, size):
            cols[k] = cols[k] - factor * factor[k : k + 1]
        pivot = inv[j : j + 1] * scale
        below = jnp.where(row > j, factor, 0.0)
        inv = jnp.where(row == j, pivot, inv - below * pivot)
    return inv[:, :size]


def small_inverse(block):
    size = block.shape[0]
    cols = columns_of(block)
    row = lax.broadcasted_iota(jnp.int32, (size, 128), 0)
    lane = lax.broadcasted_iota(jnp.int32, (size, 128), 1)
    inv = (row == lane).astype(jnp.float32)
    for j in range(size):
        scale = 1.0 / cols[j][j : j + 1]
        others = jnp.where(row == j, 0.0, cols[j])
        for k in range(j + 1, size):
            pivot = cols[k][j : j + 1] * scale
            cols[k] = jnp.where(row == j, pivot, cols[k] - others * pivot)
        pivot = inv[j : j + 1] * scale
        inv = jnp.where(row == j, pivot, inv - others * pivot)
    return inv[:, :size]


def unit(width):
    row = lax.broadcasted_iota(jnp.int32, (width, width), 0)
    lane = lax.broadcasted_iota(jnp.int32, (width, width), 1)
    return (row == lane).astype(jnp.float32)


def cholesky_inverse(gram):
    width = gram.shape[0]
    step = min(BLOCK, width)
    rest = jnp.concatenate([gram, unit(width)], axis=1)
    done = []
    for start in range(0, width, step):
        small = small_cholesky_inverse(rest[:step, start : start + step])
        lead = product(small, rest[:step], NN)
        done.append(lead[:, width:])
        if start + step < width:
            rest = rest[step:] - product(lead[:, start + step : width], lead, TN)
    return jnp.concatenate(done, axis=0)


def full_inverse(matrix):
    width = matrix.shape[0]
    step = min(BLOCK, width)
    work = jnp.concatenate([matrix, unit(width)], axis=1)
    row = lax.broadcasted_iota(jnp.int32, (width, step), 0)
    for start in range(0, width, step):
        stop = start + step
        small = small_inverse(work[start:stop, start:stop])
        lead = product(small, work[start:stop], NN)
        inside = jnp.logical_and(row >= start, row < stop)
        work = work - product(jnp.where(inside, 0.0, work[:, start:stop]), lead, NN)
        pieces = [work[:start], lead, work[stop:]]
        work = jnp.concatenate([piece for piece in pieces if piece.shape[0]], axis=0)
    return work[:, width:]


def greet(rows, cols):
    r = lax.axis_index("row")
    c = lax.axis_index("col")
    barrier = pltpu.get_barrier_semaphore()

    def body(slot, carry):
        root = slot * cols + c

        @pl.when(root != r)
        def _():
            pl.semaphore_signal(barrier, inc=1, device_id=(root, 0), device_id_type=MESH)

        @pl.when(jnp.logical_and(root != r, c != 0))
        def _():
            pl.semaphore_signal(barrier, inc=1, device_id=(root, c), device_id_type=MESH)

        return carry

    lax.fori_loop(0, rows // cols, body, 0)
    for step in range(1, cols):
        pl.semaphore_signal(
            barrier, inc=1, device_id=(r, lax.rem(c + step, cols)), device_id_type=MESH
        )


def greeted(rows, cols, sends):
    barrier = pltpu.get_barrier_semaphore()

    @pl.when(sends)
    def _():
        pl.semaphore_wait(barrier, rows - 1 + cols - 1)

    @pl.when(jnp.logical_not(sends))
    def _():
        pl.semaphore_wait(barrier, cols - 1)


def split(value):
    high = value.astype(jnp.bfloat16)
    return high, (value - high.astype(jnp.float32)).astype(jnp.bfloat16)


def product3(left, right, contract):
    def one(a, b):
        return lax.dot_general(a, b, (contract, ((), ())), preferred_element_type=jnp.float32)

    return one(left[0], right[0]) + (one(left[0], right[1]) + one(left[1], right[0]))


def panel_kernel(
    rows, cols, local_ref, change_ref,
    tiles, own, parts, slots, vecs, image, own_image, part_slots, mid, mid_slots, wide_high, wide_low,
    send_sem, recv_sem, own_send, own_recv, ex_send, ex_recv,
    im_send, im_recv, part_send, part_recv, mid_send, mid_recv,
):
    r = lax.axis_index("row")
    c = lax.axis_index("col")
    width = own.shape[0]
    is_root = c == 0
    count = rows // cols
    slot_own = r // cols
    own_col = lax.rem(r, cols)
    sends = own_col == c
    identity = unit(width)
    greet(rows, cols)

    @pl.when(is_root)
    def _():
        own[...] = local_ref[0, :, 0, :]

    greeted(rows, cols, jnp.logical_or(is_root, sends))

    @pl.when(is_root)
    def _():
        for peer in range(1, cols):
            pltpu.make_async_remote_copy(
                src_ref=own, dst_ref=own, send_sem=own_send.at[peer - 1],
                recv_sem=own_recv, device_id=(r, peer), device_id_type=MESH,
            ).start()
        spread(own, tiles, slot_own, rows, own_col, send_sem, recv_sem, False)

    for slot in range(count):
        columns = slice(slot * width, slot * width + width)
        wide_high[:, columns], wide_low[:, columns] = split(local_ref[0, :, slot, :])

    @pl.when(jnp.logical_not(is_root))
    def _():
        pltpu.make_async_remote_copy(
            src_ref=own, dst_ref=own, send_sem=own_recv,
            recv_sem=own_recv, device_id=(r, c), device_id_type=MESH,
        ).wait_recv()

    @pl.when(sends)
    def _():
        tiles[slot_own] = own[...]

    parts[...] = jnp.zeros_like(parts)

    def gram_step(slot, carry):
        tile = slot * cols + c

        @pl.when(tile != r)
        def _():
            arrive(own, tiles, slot, recv_sem)

        @pl.when(tile != 0)
        def _():
            block = tiles[slot]
            parts[0] += product(block, block, TN)

        @pl.when(tile == 1)
        def _():
            parts[1] = tiles[slot]

        return carry

    lax.fori_loop(0, count, gram_step, 0)
    for copy in exchange_start(parts, slots, ex_send, ex_recv, cols):
        copy.wait()
    sums = parts[...]
    for step in range(cols - 1):
        sums = sums + slots[step]
    inverse = cholesky_inverse(sums[0])

    def vectors(tile, block):
        keep = (tile != 0).astype(jnp.float32)
        first = (tile == 1).astype(jnp.float32)
        return product(block, inverse, NT) * keep + identity * first

    for slot in range(count):
        vecs[slot] = vectors(slot * cols + c, tiles[slot])
    flat_vec = vecs[...].reshape(count * width, width)
    vec_parts = split(flat_vec)
    mid[...] = product3((wide_high[...], wide_low[...]), vec_parts, NN)
    copies = exchange_start(mid, part_slots, part_send, part_recv, cols)
    row_vec = vectors(r, own[...])
    for copy in copies:
        copy.wait()
    total = mid[...]
    for step in range(cols - 1):
        total = total + part_slots[step]
    own_image[...] = total

    @pl.when(sends)
    def _():
        spread(own_image, image, slot_own, rows, c, im_send, im_recv, False)
        image[slot_own] = total

    coupling = full_inverse(identity + product(inverse, sums[1], NT))
    upd_rows = product(total, coupling, NN)

    mid[...] = jnp.zeros_like(mid)

    def mid_step(slot, carry):
        @pl.when(slot * cols + c != r)
        def _():
            arrive(own_image, image, slot, im_recv)

        mid[...] += product(vecs[slot], image[slot], TN)
        return carry

    lax.fori_loop(0, count, mid_step, 0)
    copies = exchange_start(mid, mid_slots, mid_send, mid_recv, cols)
    upd_cols = product3(split(image[...].reshape(count * width, width)), split(coupling), NN)
    for copy in copies:
        copy.wait()
    middle = mid[...]
    for step in range(cols - 1):
        middle = middle + mid_slots[step]
    half = 0.5 * product(coupling, product(middle, coupling, NN), TN)
    upd_rows = upd_rows - product(row_vec, half, NN)
    upd_cols = upd_cols - product3(vec_parts, split(half), NN)
    left = split(jnp.concatenate([upd_rows, row_vec], axis=1))
    right = split(jnp.concatenate([flat_vec, upd_cols], axis=1))
    change_ref[...] = product3(left, right, NT)

    @pl.when(is_root)
    def _():
        for peer in range(1, cols):
            pltpu.make_async_remote_copy(
                src_ref=own, dst_ref=own, send_sem=own_send.at[peer - 1],
                recv_sem=own_recv, device_id=(r, peer), device_id_type=MESH,
            ).wait_send()
        spread(own, tiles, slot_own, rows, own_col, send_sem, recv_sem, True)

    @pl.when(sends)
    def _():
        spread(own_image, image, slot_own, rows, c, im_send, im_recv, True)


def per_device(matrix):
    _, width, count, _ = matrix.shape
    rows = lax.axis_size("row")
    cols = lax.axis_size("col")
    dma = pltpu.SemaphoreType.DMA

    def buffer(*shape):
        return pltpu.VMEM((*shape, width, width), jnp.float32)

    change = pl.pallas_call(
        functools.partial(panel_kernel, rows, cols),
        out_shape=jax.ShapeDtypeStruct((width, count * width), jnp.float32),
        in_specs=[pl.BlockSpec(memory_space=pltpu.VMEM)],
        out_specs=pl.BlockSpec(memory_space=pltpu.VMEM),
        scratch_shapes=[
            buffer(count), buffer(), buffer(2), buffer(cols - 1, 2), buffer(count), buffer(count),
            buffer(), buffer(cols - 1), buffer(), buffer(cols - 1),
            pltpu.VMEM((width, count * width), jnp.bfloat16),
            pltpu.VMEM((width, count * width), jnp.bfloat16),
            dma((rows,)), dma((count,)), dma((cols - 1,)), dma, dma((cols - 1,)), dma((cols - 1,)),
            dma((rows,)), dma((count,)), dma((cols - 1,)), dma((cols - 1,)),
            dma((cols - 1,)), dma((cols - 1,)),
        ],
        compiler_params=pltpu.CompilerParams(
            collective_id=0, has_side_effects=True, vmem_limit_bytes=VMEM_LIMIT
        ),
    )(matrix)
    return matrix - change.reshape(matrix.shape)


def solution(mesh):
    in_specs = (P(None, "row", None, "col"),)
    out_specs = P(None, "row", None, "col")
    return jax.shard_map(
        per_device, mesh=mesh, in_specs=in_specs, out_specs=out_specs, check_vma=False
    )
```

time: 97.3 us -> 48.4 us (0.50)
  the two profiles are of different devices: /device:TPU:31 before, /device:TPU:27 now
where the time goes in v3:
time: 48.4 us; the launch traced here: 48.2 us
  Pallas kernels  46.2 us (95%)
  local copies, waits for them, and re-layouts  1.14 us (2%)
  other arithmetic  0.87 us (2%)
    pallas_call x1, Pallas kernels, per_device(): pl.pallas_call(functools.partial(panel_kernel, rows, cols), out_shape=jax...  46.2 us
    unnamed x3, local copies, waits for them, and re-layouts  1.14 us

profile of v3, /device:TPU:27, one launch (start us, length us, event | category | flops | bytes accessed | tf_op | source)
XLA Modules:
  0.0 48.2 jit_solution(9073397027245860175)
XLA Ops:
  0.0 0.0 copy-start
  0.0 1.0 %copy-done = f32[1,128,8,128]{3,2,1,0:T(8,128)S(1)} copy-done((f32[1,128,8,128]{3,2,1,0:T(8,128)S(1)}, f32[1,128,8,128]{3,2,1,0:T(8,128)}, u32[]{:S(2)}) %copy-start) | copy-done | bytes 524312
  1.0 46.2 %shard_map.17 = f32[128,1024]{1,0:T(8,128)S(1)} custom-call(f32[1,128,8,128]{3,2,1,0:T(8,128)S(1)} %copy-done), custom_call_target="tpu_custom_call" | custom-call | tf_op jit(solution)/shard_map/pallas_call | solution.py:356
  47.3 0.1 copy.2
  47.4 0.9 %bitcast_subtract_fusion = f32[1,128,8,128]{3,2,1,0:T(8,128)} fusion(f32[1,128,8,128]{3,2,1,0:T(8,128)S(1)} %copy-done, f32[1,128,8,128]{3,2,1,0:T(8,128)S(1)} %bitcast.6), kind=kLoop, calls=%fused_computation | loop fusion | flops 131072 | bytes 1572864 | tf_op jit(solution)/shard_map/sub | solution.py:374
Async XLA Ops:
  0.0 1.0 %copy-start = (f32[1,128,8,128]{3,2,1,0:T(8,128)S(1)}, f32[1,128,8,128]{3,2,1,0:T(8,128)}, u32[]{:S(2)}) copy-start(f32[1,128,8,128]{3,2,1,0:T(8,128)} %local_ref.1) | copy-start | bytes 1572868

commit v4 on v3

--- a/solution.py
+++ b/solution.py
@@ -44,16 +44,24 @@
     return copies
 
 
-def spread(source, dest, slot, rows, target_col, send_sem, recv_sem, wait):
+def plane_of(rows, cols):
+    plane = cols
+    while plane * plane < rows or rows % plane:
+        plane += cols
+    return plane
+
+
+def across(source, dest, rows, cols, target_col, send_sem, recv_sem, wait):
     r = lax.axis_index("row")
+    plane = plane_of(rows, cols)
 
     def body(step, carry):
         copy = pltpu.make_async_remote_copy(
             src_ref=source,
-            dst_ref=dest.at[slot],
-            send_sem=send_sem.at[step],
-            recv_sem=recv_sem.at[slot],
-            device_id=(lax.rem(r + step, rows), target_col),
+            dst_ref=dest.at[r // cols],
+            send_sem=send_sem.at[step * plane],
+            recv_sem=recv_sem.at[r // cols],
+            device_id=(lax.rem(r + step * plane, rows), target_col),
             device_id_type=MESH,
         )
         if wait:
@@ -62,7 +70,40 @@
             copy.start()
         return carry
 
-    lax.fori_loop(1, rows, body, 0)
+    lax.fori_loop(1, rows // plane, body, 0)
+
+
+def within(source, dest, rows, cols, send_sem, recv_sem, wait):
+    r = lax.axis_index("row")
+    c = lax.axis_index("col")
+    plane = plane_of(rows, cols)
+    base = (r // plane) * plane
+    place = lax.rem(r, plane)
+
+    def body(step, carry):
+        slot = lax.rem(r + step * plane, rows) // cols
+        if not wait:
+
+            @pl.when(step > 0)
+            def _():
+                arrive(source, dest, slot, recv_sem)
+
+        for other in range(1, plane):
+            copy = pltpu.make_async_remote_copy(
+                src_ref=dest.at[slot],
+                dst_ref=dest.at[slot],
+                send_sem=send_sem.at[step * plane + other],
+                recv_sem=recv_sem.at[slot],
+                device_id=(base + lax.rem(place + other, plane), c),
+                device_id_type=MESH,
+            )
+            if wait:
+                copy.wait_send()
+            else:
+                copy.start()
+        return carry
+
+    lax.fori_loop(0, rows // plane, body, 0)
 
 
 def arrive(source, dest, slot, recv_sem):
@@ -158,35 +199,47 @@
     r = lax.axis_index("row")
     c = lax.axis_index("col")
     barrier = pltpu.get_barrier_semaphore()
-
-    def body(slot, carry):
-        root = slot * cols + c
-
-        @pl.when(root != r)
+    plane = plane_of(rows, cols)
+    base = (r // plane) * plane
+    place = lax.rem(r, plane)
+
+    @pl.when(lax.rem(r, cols) == c)
+    def _():
+        for step in range(1, rows // plane):
+            root = lax.rem(r + step * plane, rows)
+            pl.semaphore_signal(barrier, inc=1, device_id=(root, 0), device_id_type=MESH)
+
+            @pl.when(c != 0)
+            def _():
+                pl.semaphore_signal(barrier, inc=1, device_id=(root, c), device_id_type=MESH)
+
+    for index in range(plane // cols):
+        other = index * cols + c
+
+        @pl.when(other != place)
         def _():
-            pl.semaphore_signal(barrier, inc=1, device_id=(root, 0), device_id_type=MESH)
-
-        @pl.when(jnp.logical_and(root != r, c != 0))
-        def _():
-            pl.semaphore_signal(barrier, inc=1, device_id=(root, c), device_id_type=MESH)
-
-        return carry
-
-    lax.fori_loop(0, rows // cols, body, 0)
+            pl.semaphore_signal(barrier, inc=1, device_id=(base + other, c), device_id_type=MESH)
+
     for step in range(1, cols):
         pl.semaphore_signal(
             barrier, inc=1, device_id=(r, lax.rem(c + step, cols)), device_id_type=MESH
         )
 
 
-def greeted(rows, cols, sends):
+def greeted(rows, cols, is_root, sends):
     barrier = pltpu.get_barrier_semaphore()
+    plane = plane_of(rows, cols)
+    outer = rows // plane - 1
 
     @pl.when(sends)
     def _():
-        pl.semaphore_wait(barrier, rows - 1 + cols - 1)
-
-    @pl.when(jnp.logical_not(sends))
+        pl.semaphore_wait(barrier, outer + plane - 1 + cols - 1)
+
+    @pl.when(jnp.logical_and(is_root, jnp.logical_not(sends)))
+    def _():
+        pl.semaphore_wait(barrier, outer + cols - 1)
+
+    @pl.when(jnp.logical_not(jnp.logical_or(is_root, sends)))
     def _():
         pl.semaphore_wait(barrier, cols - 1)
 
@@ -217,6 +270,8 @@
     slot_own = r // cols
     own_col = lax.rem(r, cols)
     sends = own_col == c
+    plane = plane_of(rows, cols)
+    place = lax.rem(r, plane)
     identity = unit(width)
     greet(rows, cols)
 
@@ -224,7 +279,7 @@
     def _():
         own[...] = local_ref[0, :, 0, :]
 
-    greeted(rows, cols, jnp.logical_or(is_root, sends))
+    greeted(rows, cols, is_root, sends)
 
     @pl.when(is_root)
     def _():
@@ -233,7 +288,7 @@
                 src_ref=own, dst_ref=own, send_sem=own_send.at[peer - 1],
                 recv_sem=own_recv, device_id=(r, peer), device_id_type=MESH,
             ).start()
-        spread(own, tiles, slot_own, rows, own_col, send_sem, recv_sem, False)
+        across(own, tiles, rows, cols, own_col, send_sem, recv_sem, False)
 
     for slot in range(count):
         columns = slice(slot * width, slot * width + width)
@@ -249,13 +304,14 @@
     @pl.when(sends)
     def _():
         tiles[slot_own] = own[...]
+        within(own, tiles, rows, cols, send_sem, recv_sem, False)
 
     parts[...] = jnp.zeros_like(parts)
 
     def gram_step(slot, carry):
         tile = slot * cols + c
 
-        @pl.when(tile != r)
+        @pl.when(jnp.logical_or(lax.rem(tile, plane) != place, jnp.logical_not(sends)))
         def _():
             arrive(own, tiles, slot, recv_sem)
 
@@ -299,8 +355,9 @@
 
     @pl.when(sends)
     def _():
-        spread(own_image, image, slot_own, rows, c, im_send, im_recv, False)
+        across(own_image, image, rows, cols, c, im_send, im_recv, False)
         image[slot_own] = total
+        within(own_image, image, rows, cols, im_send, im_recv, False)
 
     coupling = full_inverse(identity + product(inverse, sums[1], NT))
     upd_rows = product(total, coupling, NN)
@@ -308,7 +365,9 @@
     mid[...] = jnp.zeros_like(mid)
 
     def mid_step(slot, carry):
-        @pl.when(slot * cols + c != r)
+        away = lax.rem(slot * cols + c, plane) != place
+
+        @pl.when(jnp.logical_or(away, jnp.logical_not(sends)))
         def _():
             arrive(own_image, image, slot, im_recv)
 
@@ -337,11 +396,13 @@
                 src_ref=own, dst_ref=own, send_sem=own_send.at[peer - 1],
                 recv_sem=own_recv, device_id=(r, peer), device_id_type=MESH,
             ).wait_send()
-        spread(own, tiles, slot_own, rows, own_col, send_sem, recv_sem, True)
+        across(own, tiles, rows, cols, own_col, send_sem, recv_sem, True)
 
     @pl.when(sends)
     def _():
-        spread(own_image, image, slot_own, rows, c, im_send, im_recv, True)
+        within(own, tiles, rows, cols, send_sem, recv_sem, True)
+        across(own_image, image, rows, cols, c, im_send, im_recv, True)
+        within(own_image, image, rows, cols, im_send, im_recv, True)
 
 
 def per_device(matrix):

time: 48.4 us -> 45.8 us (0.946)
  the two profiles are of different devices: /device:TPU:27 before, /device:TPU:0 now
where the time goes in v4:
time: 45.8 us; the launch traced here: 45.6 us
  Pallas kernels  43.6 us (95%)
  local copies, waits for them, and re-layouts  1.14 us (2%)
  other arithmetic  0.87 us (2%)
    pallas_call x1, Pallas kernels, per_device(): pl.pallas_call(functools.partial(panel_kernel, rows, cols), out_shape=jax...  43.6 us
    unnamed x3, local copies, waits for them, and re-layouts  1.14 us

profile of v4, /device:TPU:0, one launch (start us, length us, event | category | flops | bytes accessed | tf_op | source)
XLA Modules:
  0.0 45.6 jit_solution(3113381546722287418)
XLA Ops:
  0.0 0.0 copy-start
  0.0 1.0 %copy-done = f32[1,128,8,128]{3,2,1,0:T(8,128)S(1)} copy-done((f32[1,128,8,128]{3,2,1,0:T(8,128)S(1)}, f32[1,128,8,128]{3,2,1,0:T(8,128)}, u32[]{:S(2)}) %copy-start) | copy-done | bytes 524312
  1.0 43.6 %shard_map.17 = f32[128,1024]{1,0:T(8,128)S(1)} custom-call(f32[1,128,8,128]{3,2,1,0:T(8,128)S(1)} %copy-done), custom_call_target="tpu_custom_call" | custom-call | tf_op jit(solution)/shard_map/pallas_call | solution.py:417
  44.7 0.1 copy.2
  44.8 0.9 %bitcast_subtract_fusion = f32[1,128,8,128]{3,2,1,0:T(8,128)} fusion(f32[1,128,8,128]{3,2,1,0:T(8,128)S(1)} %copy-done, f32[1,128,8,128]{3,2,1,0:T(8,128)S(1)} %bitcast.6), kind=kLoop, calls=%fused_computation | loop fusion | flops 131072 | bytes 1572864 | tf_op jit(solution)/shard_map/sub | solution.py:435
Async XLA Ops:
  0.0 1.0 %copy-start = (f32[1,128,8,128]{3,2,1,0:T(8,128)S(1)}, f32[1,128,8,128]{3,2,1,0:T(8,128)}, u32[]{:S(2)}) copy-start(f32[1,128,8,128]{3,2,1,0:T(8,128)} %local_ref.1) | copy-start | bytes 1572868

commit v5 on v4

--- a/solution.py
+++ b/solution.py
@@ -306,27 +306,24 @@
         tiles[slot_own] = own[...]
         within(own, tiles, rows, cols, send_sem, recv_sem, False)
 
-    parts[...] = jnp.zeros_like(parts)
-
-    def gram_step(slot, carry):
-        tile = slot * cols + c
-
-        @pl.when(jnp.logical_or(lax.rem(tile, plane) != place, jnp.logical_not(sends)))
-        def _():
-            arrive(own, tiles, slot, recv_sem)
-
-        @pl.when(tile != 0)
-        def _():
-            block = tiles[slot]
-            parts[0] += product(block, block, TN)
-
-        @pl.when(tile == 1)
-        def _():
-            parts[1] = tiles[slot]
-
-        return carry
-
-    lax.fori_loop(0, count, gram_step, 0)
+    def arrive_rest(source, dest, sem):
+        def body(slot, carry):
+            away = lax.rem(slot * cols + c, plane) != place
+
+            @pl.when(jnp.logical_or(away, jnp.logical_not(sends)))
+            def _():
+                arrive(source, dest, slot, sem)
+
+            return carry
+
+        lax.fori_loop(0, count, body, 0)
+
+    arrive_rest(own, tiles, recv_sem)
+    flat = tiles[...].reshape(count * width, width)
+    place_row = lax.broadcasted_iota(jnp.int32, flat.shape, 0)
+    flat = jnp.where(jnp.logical_and(place_row < width, c == 0), 0.0, flat)
+    parts[0] = product(flat, flat, TN)
+    parts[1] = jnp.where(c == 1 % cols, tiles[1 // cols], 0.0)
     for copy in exchange_start(parts, slots, ex_send, ex_recv, cols):
         copy.wait()
     sums = parts[...]
@@ -339,8 +336,8 @@
         first = (tile == 1).astype(jnp.float32)
         return product(block, inverse, NT) * keep + identity * first
 
-    for slot in range(count):
-        vecs[slot] = vectors(slot * cols + c, tiles[slot])
+    vecs[...] = product(flat, inverse, NT).reshape(vecs.shape)
+    vecs[1 // cols] += identity * (c == 1 % cols).astype(jnp.float32)
     flat_vec = vecs[...].reshape(count * width, width)
     vec_parts = split(flat_vec)
     mid[...] = product3((wide_high[...], wide_low[...]), vec_parts, NN)
@@ -362,21 +359,11 @@
     coupling = full_inverse(identity + product(inverse, sums[1], NT))
     upd_rows = product(total, coupling, NN)
 
-    mid[...] = jnp.zeros_like(mid)
-
-    def mid_step(slot, carry):
-        away = lax.rem(slot * cols + c, plane) != place
-
-        @pl.when(jnp.logical_or(away, jnp.logical_not(sends)))
-        def _():
-            arrive(own_image, image, slot, im_recv)
-
-        mid[...] += product(vecs[slot], image[slot], TN)
-        return carry
-
-    lax.fori_loop(0, count, mid_step, 0)
+    arrive_rest(own_image, image, im_recv)
+    flat_image = split(image[...].reshape(count * width, width))
+    mid[...] = product3(vec_parts, flat_image, TN)
     copies = exchange_start(mid, mid_slots, mid_send, mid_recv, cols)
-    upd_cols = product3(split(image[...].reshape(count * width, width)), split(coupling), NN)
+    upd_cols = product3(flat_image, split(coupling), NN)
     for copy in copies:
         copy.wait()
     middle = mid[...]

time: 45.8 us -> 43.9 us (0.959)
  Pallas kernels: 43.6 us -> 41.7 us
    pallas_call x1, Pallas kernels: 43.6 us -> 41.7 us  [per_device(): pl.pallas_call(functools.partial(panel_kernel, rows, cols), out_shape=jax...]
where the time goes in v5:
time: 43.9 us; the launch traced here: 43.7 us
  Pallas kernels  41.7 us (95%)
  local copies, waits for them, and re-layouts  1.14 us (3%)
  other arithmetic  0.87 us (2%)
    pallas_call x1, Pallas kernels, per_device(): pl.pallas_call(functools.partial(panel_kernel, rows, cols), out_shape=jax...  41.7 us
    unnamed x3, local copies, waits for them, and re-layouts  1.14 us

profile of v5, /device:TPU:0, one launch (start us, length us, event | category | flops | bytes accessed | tf_op | source)
XLA Modules:
  0.0 43.7 jit_solution(10209647742068488992)
XLA Ops:
  0.0 0.0 copy-start
  0.0 1.0 %copy-done = f32[1,128,8,128]{3,2,1,0:T(8,128)S(1)} copy-done((f32[1,128,8,128]{3,2,1,0:T(8,128)S(1)}, f32[1,128,8,128]{3,2,1,0:T(8,128)}, u32[]{:S(2)}) %copy-start) | copy-done | bytes 524312
  1.0 41.7 %shard_map.17 = f32[128,1024]{1,0:T(8,128)S(1)} custom-call(f32[1,128,8,128]{3,2,1,0:T(8,128)S(1)} %copy-done), custom_call_target="tpu_custom_call" | custom-call | tf_op jit(solution)/shard_map/pallas_call | solution.py:404
  42.7 0.1 copy.2
  42.8 0.9 %bitcast_subtract_fusion = f32[1,128,8,128]{3,2,1,0:T(8,128)} fusion(f32[1,128,8,128]{3,2,1,0:T(8,128)S(1)} %copy-done, f32[1,128,8,128]{3,2,1,0:T(8,128)S(1)} %bitcast.6), kind=kLoop, calls=%fused_computation | loop fusion | flops 131072 | bytes 1572864 | tf_op jit(solution)/shard_map/sub | solution.py:422
Async XLA Ops:
  0.0 1.0 %copy-start = (f32[1,128,8,128]{3,2,1,0:T(8,128)S(1)}, f32[1,128,8,128]{3,2,1,0:T(8,128)}, u32[]{:S(2)}) copy-start(f32[1,128,8,128]{3,2,1,0:T(8,128)} %local_ref.1) | copy-start | bytes 1572868

commit v6 on v5

--- a/solution.py
+++ b/solution.py
@@ -117,7 +117,7 @@
     ).wait_recv()
 
 
-BLOCK = 16
+BLOCK = 32
 
 
 def columns_of(block):

time: 43.9 us -> 41.9 us (0.954)
  Pallas kernels: 41.7 us -> 39.8 us
    pallas_call x1, Pallas kernels: 41.7 us -> 39.8 us  [per_device(): pl.pallas_call(functools.partial(panel_kernel, rows, cols), out_shape=jax...]
where the time goes in v6:
time: 41.9 us; the launch traced here: 41.8 us
  Pallas kernels  39.8 us (95%)
  local copies, waits for them, and re-layouts  1.14 us (3%)
  other arithmetic  0.87 us (2%)
    pallas_call x1, Pallas kernels, per_device(): pl.pallas_call(functools.partial(panel_kernel, rows, cols), out_shape=jax...  39.8 us
    unnamed x3, local copies, waits for them, and re-layouts  1.14 us
    sub x1, other arithmetic, per_device(): return matrix - change.reshape(matrix.shape)  0.87 us

profile of v6, /device:TPU:0, one launch (start us, length us, event | category | flops | bytes accessed | tf_op | source)
XLA Modules:
  0.0 41.8 jit_solution(12482014398826007888)
XLA Ops:
  0.0 0.0 copy-start
  0.0 1.0 %copy-done = f32[1,128,8,128]{3,2,1,0:T(8,128)S(1)} copy-done((f32[1,128,8,128]{3,2,1,0:T(8,128)S(1)}, f32[1,128,8,128]{3,2,1,0:T(8,128)}, u32[]{:S(2)}) %copy-start) | copy-done | bytes 524312
  1.0 39.8 %shard_map.17 = f32[128,1024]{1,0:T(8,128)S(1)} custom-call(f32[1,128,8,128]{3,2,1,0:T(8,128)S(1)} %copy-done), custom_call_target="tpu_custom_call" | custom-call | tf_op jit(solution)/shard_map/pallas_call | solution.py:404
  40.8 0.1 copy.2
  40.9 0.9 %bitcast_subtract_fusion = f32[1,128,8,128]{3,2,1,0:T(8,128)} fusion(f32[1,128,8,128]{3,2,1,0:T(8,128)S(1)} %copy-done, f32[1,128,8,128]{3,2,1,0:T(8,128)S(1)} %bitcast.6), kind=kLoop, calls=%fused_computation | loop fusion | flops 131072 | bytes 1572864 | tf_op jit(solution)/shard_map/sub | solution.py:422
Async XLA Ops:
  0.0 1.0 %copy-start = (f32[1,128,8,128]{3,2,1,0:T(8,128)S(1)}, f32[1,128,8,128]{3,2,1,0:T(8,128)}, u32[]{:S(2)}) copy-start(f32[1,128,8,128]{3,2,1,0:T(8,128)} %local_ref.1) | copy-start | bytes 1572868
